TPU v7x, 256 devices: a whole 4x4x8 slice. The times are simulated.
256 devices in a mesh: replica: 2 (over core), fsdp: 128 (over x, y, z).
Axes of the slice: x: 4, y: 4, z: 8, core: 2. Of those that a mesh axis runs over, the one named last changes fastest.
Arguments:
- grad_parts: bfloat16 [2, 512, 16, 8192], P('replica', 'fsdp'), may hold values from -1.5 to 1.5
- left_basis: float32 [256, 512, 512], P(('replica', 'fsdp')), may hold values from -0.25 to 0.25
- right_basis: float32 [256, 512, 512], P(('replica', 'fsdp')), may hold values from -0.25 to 0.25
- first_moment: float32 [256, 512, 512], P(('replica', 'fsdp')), may hold values from -1.5 to 1.5
- second_moment: float32 [256, 512, 512], P(('replica', 'fsdp')), may hold values from 0.001 to 0.1
- left_factor: float32 [256, 512, 512], P(('replica', 'fsdp')), may hold values from -1.5 to 1.5
- right_factor: float32 [256, 512, 512], P(('replica', 'fsdp')), may hold values from -1.5 to 1.5
- owner_table: int32 [2, 128], replicated, may hold values from 0 to 127, each once within a row
Outputs:
- update: float32 [512, 16, 8192], P('fsdp', 'replica')
- new_first: float32 [256, 512, 512], P(('replica', 'fsdp'))
- new_second: float32 [256, 512, 512], P(('replica', 'fsdp'))
- new_left: float32 [256, 512, 512], P(('replica', 'fsdp'))
- new_right: float32 [256, 512, 512], P(('replica', 'fsdp'))
Inputs may be any that keep to these rules, and one draw needn't show every extreme that they name: Each row of owner_table names every block of its half once.
All inputs are finite; a program needn't handle non-finite values.
Results may differ from a plain program's by a relative error of at most 0.0003.
Values may be sent and summed in bfloat16 or wider, within the bound.
A program may use at most 64 MiB of HBM per device.

v0:
```python
import functools

import jax
import jax.numpy as jnp
from jax import lax
from jax.experimental import pallas as pl
from jax.experimental.pallas import tpu as pltpu
from jax.sharding import PartitionSpec as P

MESH = pl.DeviceIdType.MESH
N = 128
B = 512
TINY = 1e-33
FAR_Z = (4, 3, 5, 2, 6, 1, 7, 0)
F32, BF16, I32 = jnp.float32, jnp.bfloat16, jnp.int32
CHUNKS = 4
WIDE = 8192 // CHUNKS


def far_x(plane):
    return jnp.where(plane == 0, 2, jnp.where(plane == 3, 0, 2 * plane - 1))


def turned(step, size, rep):
    return lax.rem(jnp.where(rep == 0, step, size - step), size)


def split(x):
    high = x.astype(BF16)
    return high, (x - high.astype(F32)).astype(BF16)


def dot3(a, b, dims=((1,), (0,))):
    one = functools.partial(
        lax.dot_general,
        dimension_numbers=(dims, ((), ())),
        preferred_element_type=F32,
    )
    return one(a[0], b[0]) + (one(a[0], b[1]) + one(a[1], b[0]))


def dot3_few(a, b):
    both = jnp.dot(
        jnp.concatenate(a, axis=0), b[0], preferred_element_type=F32
    )
    count = a[0].shape[0]
    cross = jnp.dot(a[0], b[1], preferred_element_type=F32)
    return both[:count] + (both[count:] + cross)


def pack(q):
    return (q[:, :256] << 16) | (q[:, 256:] & 0xFFFF)


def unpack(w):
    return w >> 16, (w << 16) >> 16


def rows(start, size=8):
    return pl.ds(pl.multiple_of(start, 8), size)


def step_kernel(
    g_hbm, l_hbm, r_hbm, m_hbm, v_hbm, lf_hbm, rf_hbm, table_hbm,
    back_words, back_scales, new_first, new_second, new_left, new_right,
    g, l, r, m, v, lf, rf, table,
    own, sib_out, sib_in, pieces, scales, out_words, out_scales, in_words, in_scales,
    blocks, lh, ll, lth, ltl, rh, rl, rth, rtl, bh, bl, wh, wl, ret_words, ret_scales,
    met, g_sem, in_sem, sib_send, sib_recv, fwd_send, fwd_recv, bwd_send, bwd_recv,
):
    rep = lax.axis_index("replica")
    me = lax.axis_index("fsdp")
    wides = [pl.ds(j * WIDE, WIDE) for j in range(CHUNKS)]
    loads = [
        pltpu.make_async_copy(g_hbm.at[0, :, :, w], g.at[:, :, w], g_sem.at[j])
        for j, w in enumerate(wides)
    ]
    pairs = (
        (table_hbm, table), (l_hbm.at[0], l), (r_hbm.at[0], r), (m_hbm.at[0], m),
        (v_hbm.at[0], v), (lf_hbm.at[0], lf), (rf_hbm.at[0], rf),
    )
    others = [
        pltpu.make_async_copy(a, b, in_sem.at[j]) for j, (a, b) in enumerate(pairs)
    ]
    for copy in loads:
        copy.start()

    x, y, z = me // 32, lax.rem(me // 8, 4), lax.rem(me, 8)
    line = [x * 32 + y * 8 + lax.rem(z + d, 8) for d in range(1, 8)]
    slab = [
        lax.rem(x + d // 4, 4) * 32 + lax.rem(y + d, 4) * 8 + z for d in range(1, 16)
    ]
    barrier = pltpu.get_barrier_semaphore()
    for peer in [(1 - rep, me)] + [(rep, q) for q in line + slab]:
        pl.semaphore_signal(barrier, inc=1, device_id=peer, device_id_type=MESH)
    for copy in others:
        copy.start()

    def part(c):
        cols = pl.ds(c * B, B)
        for pair in range(2):
            sent = []
            for i in (2 * pair, 2 * pair + 1):
                x = g[i, :, cols].astype(F32)
                low, high = x[:8], x[8:]
                own[i, :, cols] = jnp.where(rep == 0, low, high)
                sent.append(jnp.where(rep == 0, high, low))
            sib_out[pair, :, cols] = jnp.concatenate(sent, axis=0).astype(BF16)

    exchange = [
        pltpu.make_async_remote_copy(
            src_ref=sib_out.at[:, :, w],
            dst_ref=sib_in.at[:, :, w],
            send_sem=sib_send.at[j],
            recv_sem=sib_recv.at[j],
            device_id=(1 - rep, me),
            device_id_type=MESH,
        )
        for j, w in enumerate(wides)
    ]
    for j, copy in enumerate(loads):
        copy.wait()
        for c in range(j * 16 // CHUNKS, (j + 1) * 16 // CHUNKS):
            part(c)
        if j == 0:
            pl.semaphore_wait(barrier, 23)
        exchange[j].start()
        if j == 0:
            for q in line:
                pl.semaphore_signal(
                    met, inc=1, device_id=(rep, q), device_id_type=MESH
                )

    def code(c):
        cols = pl.ds(c * B, B)
        xs = []
        for pair in range(2):
            y = sib_in[pair, :, cols].astype(F32)
            xs.append(own[2 * pair, :, cols] + y[:8])
            xs.append(own[2 * pair + 1, :, cols] + y[8:])
        top = functools.reduce(jnp.maximum, [jnp.abs(x) for x in xs])
        top = jnp.maximum(jnp.max(top, axis=1, keepdims=True), TINY)
        inverse = 32767.0 / top
        for i, x in enumerate(xs):
            w = pack(jnp.round(x * inverse).astype(I32))
            for half in range(2):
                pieces[pl.ds(c * 8 + i * 2 + half, 8, stride=128), :] = w[
                    :, half * 128 : half * 128 + 128
                ]
        scales[pl.ds(c, 8, stride=16), :] = jnp.broadcast_to(
            top * (1.0 / 32767.0), (8, 128)
        )

    for j, copy in enumerate(exchange):
        copy.wait()
        for c in range(j * 16 // CHUNKS, (j + 1) * 16 // CHUNKS):
            code(c)

    ends = [lax.rem(z + turned(d, 8, rep), 8) for d in FAR_Z]

    def partners(block):
        at_y = lax.rem(y + turned(far_x(lax.rem(block, 4)), 4, rep), 4)
        at_x = lax.rem(x + turned(far_x(block // 4), 4, rep), 4)
        return [at_x * 32 + at_y * 8 + end for end in ends]

    def gather(block, found):
        stock = pieces.reshape(N, 8, 128)
        picked = []
        for q in found:
            k = table[rep, q]
            picked.append((stock[k], scales[pl.ds(k, 1), :]))
        for u, (word, scale) in enumerate(picked):
            out_words[rows(block * 64 + u * 8), :] = word
            out_scales[block * 8 + u] = scale

    def sends(words, lines, to_words, to_lines, send_sem, recv_sem, plane, forward):
        def one(block, found, count):
            for u, q in enumerate(found[:count]):
                slot = block * 8 + u if forward else q
                pltpu.make_async_remote_copy(
                    src_ref=words.at[rows(slot * 8)],
                    dst_ref=to_words.at[rows(me * 8)],
                    send_sem=send_sem.at[0],
                    recv_sem=recv_sem.at[0],
                    device_id=(rep, q),
                    device_id_type=MESH,
                ).start()
                pltpu.make_async_remote_copy(
                    src_ref=lines.at[slot],
                    dst_ref=to_lines.at[me],
                    send_sem=send_sem.at[1],
                    recv_sem=recv_sem.at[1],
                    device_id=(rep, q),
                    device_id_type=MESH,
                ).start()

        def whole(block, c, count=8):
            found = partners(block)
            if forward:
                gather(block, found)
            one(block, found, count)
            return c

        lax.fori_loop(plane * 4, min(plane * 4 + 4, 15), whole, 0)
        if plane == 3:
            whole(jnp.int32(15), 0, 7)

    others[0].wait()
    pl.semaphore_wait(met, 7)
    for plane in range(4):
        sends(
            out_words, out_scales, in_words, in_scales,
            fwd_send, fwd_recv.at[plane], plane, True,
        )
    in_words[rows(me * 8), :] = out_words[rows(8 * (N - 1)), :]
    in_scales[me] = out_scales[N - 1]

    def away(plane):
        return lax.rem(x + 4 - turned(far_x(plane), 4, rep), 4)

    for copy in others[1:]:
        copy.wait()
    for full, h, w in ((l, lh, ll), (r, rh, rl)):
        h[...], w[...] = split(full[...])
    rth[...], rtl[...] = split(r[...].T)
    for plane in range(4):
        cols = slice(plane * 128, plane * 128 + 128)
        lth[:, cols], ltl[:, cols] = split(l[rows(away(plane) * 128, 128), :].T)

    def arrived(sems, words, lines, count):
        pltpu.make_async_copy(
            words.at[rows(0, 8 * count)], words.at[rows(0, 8 * count)], sems.at[0]
        ).wait()
        pltpu.make_async_copy(
            lines.at[pl.ds(0, count)], lines.at[pl.ds(0, count)], sems.at[1]
        ).wait()

    upper = lax.broadcasted_iota(I32, (8, 128), 0) < 4

    def decode(j):
        scale = jnp.where(
            upper,
            jnp.broadcast_to(in_scales[2 * j], (8, 128)),
            jnp.broadcast_to(in_scales[2 * j + 1], (8, 128)),
        )
        for half in range(2):
            a, b = unpack(in_words[pl.ds(j * 16 + half, 8, stride=2), :])
            for q, col in ((a, half), (b, half + 2)):
                blocks[rows(j * 8), col * 128 : col * 128 + 128] = q.astype(F32) * scale

    for plane in range(4):
        arrived(fwd_recv.at[plane], in_words, in_scales, 31 if plane == 3 else 32)
        first = away(plane) * 16
        for j in range(16):
            decode(first + j)
        some, here = rows(first * 8, 128), slice(plane * 128, plane * 128 + 128)
        high, low = split(blocks[some, :])
        bh[some, :], bl[some, :] = high, low
        wh[here, :], wl[here, :] = split(
            dot3_few((high, low), (rh[...], rl[...]))
        )
        if plane == 2:
            new_first[...] = dot3(
                (lth[:, :384], ltl[:, :384]), (wh[:384, :], wl[:384, :])
            )
    tail = wh[384:, :]
    rotated = new_first[...] + (
        jnp.dot(
            jnp.concatenate([lth[:, 384:], ltl[:, 384:]], axis=1),
            jnp.concatenate([tail, tail], axis=0),
            preferred_element_type=F32,
        )
        + jnp.dot(lth[:, 384:], wl[384:, :], preferred_element_type=F32)
    )
    first = 0.95 * m[...] + 0.05 * rotated
    second = 0.95 * v[...] + 0.05 * rotated * rotated
    new_first[...] = first
    new_second[...] = second
    wh[...], wl[...] = split(first / (jnp.sqrt(second) + 1e-08))

    def encode(j, x):
        top = jnp.max(jnp.max(jnp.abs(x), axis=0, keepdims=True), axis=1, keepdims=True)
        top = jnp.maximum(top, TINY)
        w = pack(jnp.round(x * (32767.0 / top)).astype(I32))
        for half in range(2):
            ret_words[pl.ds(j * 16 + half, 8, stride=2), :] = w[
                :, half * 128 : half * 128 + 128
            ]
        scale = jnp.broadcast_to(top * (1.0 / 32767.0), (1, 128))
        ret_scales[2 * j] = scale
        ret_scales[2 * j + 1] = scale

    for plane in range(4):
        first = lax.rem(x + turned(far_x(plane), 4, rep), 4) * 16
        some = rows(first * 8, 128)
        part_left = split(dot3_few((lh[some, :], ll[some, :]), (wh[...], wl[...])))
        back = dot3_few(part_left, (rth[...], rtl[...]))
        for j in range(16):
            encode(first + j, back[j * 8 : j * 8 + 8, :])
        sends(
            ret_words, ret_scales, back_words, back_scales,
            bwd_send, bwd_recv, plane, False,
        )
    back_words[rows(me * 8), :] = ret_words[rows(me * 8), :]
    back_scales[me] = ret_scales[me]

    pair = (bh[...], bl[...])
    new_left[...] = 0.95 * lf[...] + 0.05 * dot3(pair, pair, ((1,), (1,)))
    new_right[...] = 0.95 * rf[...] + 0.05 * dot3(pair, pair, ((0,), (0,)))

    arrived(fwd_send, out_words, out_scales, N - 1)
    arrived(bwd_send, ret_words, ret_scales, N - 1)
    arrived(bwd_recv, back_words, back_scales, N - 1)


def write_kernel(
    words, lines, first, second, left, right, table_hbm,
    update_hbm, first_hbm, second_hbm, left_hbm, right_hbm,
    pieces, scales, update, table, sems,
):
    rep = lax.axis_index("replica")
    fetch = pltpu.make_async_copy(table_hbm, table, sems.at[8])
    fetch.start()
    pairs = ((first, first_hbm), (second, second_hbm), (left, left_hbm), (right, right_hbm))
    copies = [
        pltpu.make_async_copy(a, b.at[0], sems.at[j]) for j, (a, b) in enumerate(pairs)
    ]
    for copy in copies:
        copy.start()
    fetch.wait()

    def place(q, c):
        k = table[rep, q]
        pieces[rows(k * 8), :] = words[rows(q * 8), :]
        scales[pl.ds(k, 1), :] = lines[q]
        return c

    lax.fori_loop(0, N, place, 0, unroll=8)

    def decode(c):
        scale = scales[pl.ds(c, 8, stride=16), :]
        for i in range(4):
            for half in range(2):
                w = pieces[pl.ds(c * 8 + i * 2 + half, 8, stride=128), :]
                for q, col in zip(unpack(w), (half, half + 2)):
                    cols = pl.ds(c * B + col * 128, 128)
                    update[i, :, cols] = q.astype(F32) * scale

    for j in range(CHUNKS):
        for c in range(j * 16 // CHUNKS, (j + 1) * 16 // CHUNKS):
            decode(c)
        w = pl.ds(j * WIDE, WIDE)
        copies.append(
            pltpu.make_async_copy(
                update.at[:, :, w], update_hbm.at[:, :, w], sems.at[4 + j]
            )
        )
        copies[-1].start()
    for copy in copies:
        copy.wait()


def body(grad_parts, left_basis, right_basis, first, second, left, right, table):
    hbm = pl.BlockSpec(memory_space=pltpu.HBM)
    vmem = pl.BlockSpec(memory_space=pltpu.VMEM)
    table_smem = pltpu.SMEM((2, N), I32)
    square = jax.ShapeDtypeStruct((B, B), F32)
    halves = [pltpu.VMEM((B, B), BF16)] * 12
    words, lines = pltpu.VMEM((N * 8, 128), I32), pltpu.VMEM((N, 1, 128), F32)
    dma = pltpu.SemaphoreType.DMA
    mids = pl.pallas_call(
        step_kernel,
        out_shape=(
            jax.ShapeDtypeStruct((N * 8, 128), I32),
            jax.ShapeDtypeStruct((N, 1, 128), F32),
            square, square, square, square,
        ),
        in_specs=[hbm] * 8,
        out_specs=(vmem,) * 6,
        scratch_shapes=[
            pltpu.VMEM((4, 16, 8192), BF16),
            *[pltpu.VMEM((B, B), F32)] * 6,
            table_smem,
            pltpu.VMEM((4, 8, 8192), F32),
            pltpu.VMEM((2, 16, 8192), BF16),
            pltpu.VMEM((2, 16, 8192), BF16),
            words, pltpu.VMEM((N, 128), F32), words, lines, words, lines,
            pltpu.VMEM((B, B), F32),
            *halves,
            words, lines,
            pltpu.SemaphoreType.REGULAR,
            dma((CHUNKS,)), dma((7,)), dma((CHUNKS,)), dma((CHUNKS,)),
            dma((2,)), dma((4, 2)), dma((2,)), dma((2,)),
        ],
        compiler_params=pltpu.CompilerParams(
            collective_id=0, has_side_effects=True, vmem_limit_bytes=49 * 2**20
        ),
    )(grad_parts, left_basis, right_basis, first, second, left, right, table)
    whole = jax.ShapeDtypeStruct((1, B, B), F32)
    return pl.pallas_call(
        write_kernel,
        out_shape=(
            jax.ShapeDtypeStruct((4, 8, 8192), F32), whole, whole, whole, whole
        ),
        in_specs=[vmem] * 6 + [hbm],
        out_specs=(hbm,) * 5,
        scratch_shapes=[
            words, pltpu.VMEM((N, 128), F32), pltpu.VMEM((4, 8, 8192), F32),
            table_smem, dma((9,)),
        ],
        compiler_params=pltpu.CompilerParams(vmem_limit_bytes=16 * 2**20),
    )(*mids, table)


def solution(mesh):
    owned = P(("replica", "fsdp"), None, None)
    return jax.shard_map(
        body,
        mesh=mesh,
        in_specs=(P("replica", "fsdp", None, None),) + (owned,) * 6 + (P(),),
        out_specs=(P("fsdp", "replica", None),) + (owned,) * 4,
        check_vma=False,
    )
```

profile of v0, /device:TPU:4, one launch (start us, length us, event | category | flops | bytes accessed | tf_op | source)
XLA Modules:
  0.0 48.4 jit_solution(15286530245490714903)
XLA Ops:
  0.6 0.0 copy-start
  0.6 0.7 %copy-done = s32[2,128]{1,0:T(2,128)S(1)} copy-done((s32[2,128]{1,0:T(2,128)S(1)}, s32[2,128]{1,0:T(2,128)}, u32[]{:S(2)}) %copy-start) | copy-done | bytes 1048
  1.3 44.7 %shard_map.119 = (s32[1024,128]{1,0:T(8,128)S(1)}, f32[128,1,128]{2,1,0:T(1,128)S(1)}, f32[512,512]{1,0:T(8,128)S(1)}, f32[512,512]{1,0:T(8,128)S(1)}, f32[512,512]{1,0:T(8,128)S(1)}, /*index=5*/f32[512,512]{1,0:T(8,128)S(1)}) custom-call(bf16[1,4,16,8192]{3,2,1,0:T(8,128)(2,1)} %g_hbm.1, f32[1,512,512]{2,1,0:T(8,128)} %l_hbm.1, f32[1,512,512]{2,1,0:T(8,128)} %r_hbm.1, ...), custom_call_target="tpu_custom_call" | custom-call | tf_op jit(solution)/shard_map/pallas_call | solution.py:371
  46.0 2.4 %shard_map.120 = (f32[4,8,8192]{2,1,0:T(8,128)}, f32[1,512,512]{2,1,0:T(8,128)}, f32[1,512,512]{2,1,0:T(8,128)}, f32[1,512,512]{2,1,0:T(8,128)}, f32[1,512,512]{2,1,0:T(8,128)}) custom-call(s32[1024,128]{1,0:T(8,128)S(1)} %get-tuple-element.11.words, f32[128,1,128]{2,1,0:T(1,128)S(1)} %get-tuple-element.12.lines, f32[512,512]{1,0:T(8,128)S(1)} %get-tuple-element.13.first, ...), custom_call_target="tpu_custom_call" | custom-call | tf_op jit(solution)/shard_map/pallas_call | solution.py:400
Async XLA Ops:
  0.6 0.7 %copy-start = (s32[2,128]{1,0:T(2,128)S(1)}, s32[2,128]{1,0:T(2,128)}, u32[]{:S(2)}) copy-start(s32[2,128]{1,0:T(2,128)} %table_hbm.3) | copy-start | bytes 3076
where the time goes:
time: 48.5 us; the launch traced here: 48.4 us
  Pallas kernels  47.1 us (97%)
  local copies, waits for them, and re-layouts  0.67 us (1%)
  between operations  0.65 us (1%)
    pallas_call x1, Pallas kernels, body(): pl.pallas_call(step_kernel, out_shape=(jax.ShapeDtypeStruct((N * 8, 128),...  44.7 us
    pallas_call x1, Pallas kernels, body(): pl.pallas_call(write_kernel, out_shape=(jax.ShapeDtypeStruct((4, 8, 8192)...  2.4 us

commit v1 on v0

--- a/solution.py
+++ b/solution.py
@@ -1,4 +1,5 @@
 import functools
+import math
 
 import jax
 import jax.numpy as jnp
@@ -11,6 +12,9 @@
 N = 128
 B = 512
 TINY = 1e-33
+MOST, LEAST = math.log2(3.0), -126.0
+COARSE = 24.0
+FINE = (32767 - COARSE * (MOST - 28 - LEAST)) / 28
 FAR_Z = (4, 3, 5, 2, 6, 1, 7, 0)
 F32, BF16, I32 = jnp.float32, jnp.bfloat16, jnp.int32
 CHUNKS = 4
@@ -48,6 +52,22 @@
     return both[:count] + (both[count:] + cross)
 
 
+def log_code(x):
+    size = jnp.log2(jnp.maximum(jnp.abs(x), 2.0**LEAST))
+    code = jnp.maximum(FINE * (size - MOST) + 32767.0, COARSE * (size - LEAST))
+    code = jnp.round(code).astype(I32)
+    return jnp.where(x < 0, -code, code)
+
+
+def log_value(code):
+    steps = jnp.abs(code).astype(F32)
+    size = jnp.minimum(
+        (steps - 32767.0) * (1 / FINE) + MOST, steps * (1 / COARSE) + LEAST
+    )
+    size = jnp.exp2(size)
+    return jnp.where(code == 0, 0.0, jnp.where(code < 0, -size, size))
+
+
 def pack(q):
     return (q[:, :256] << 16) | (q[:, 256:] & 0xFFFF)
 
@@ -64,7 +84,7 @@
     g_hbm, l_hbm, r_hbm, m_hbm, v_hbm, lf_hbm, rf_hbm, table_hbm,
     back_words, back_scales, new_first, new_second, new_left, new_right,
     g, l, r, m, v, lf, rf, table,
-    own, sib_out, sib_in, pieces, scales, out_words, out_scales, in_words, in_scales,
+    own, sib_out, sib_in, pieces, out_words, in_words,
     blocks, lh, ll, lth, ltl, rh, rl, rth, rtl, bh, bl, wh, wl, ret_words, ret_scales,
     met, g_sem, in_sem, sib_send, sib_recv, fwd_send, fwd_recv, bwd_send, bwd_recv,
 ):
@@ -138,18 +158,12 @@
             y = sib_in[pair, :, cols].astype(F32)
             xs.append(own[2 * pair, :, cols] + y[:8])
             xs.append(own[2 * pair + 1, :, cols] + y[8:])
-        top = functools.reduce(jnp.maximum, [jnp.abs(x) for x in xs])
-        top = jnp.maximum(jnp.max(top, axis=1, keepdims=True), TINY)
-        inverse = 32767.0 / top
         for i, x in enumerate(xs):
-            w = pack(jnp.round(x * inverse).astype(I32))
+            w = pack(log_code(x))
             for half in range(2):
                 pieces[pl.ds(c * 8 + i * 2 + half, 8, stride=128), :] = w[
                     :, half * 128 : half * 128 + 128
                 ]
-        scales[pl.ds(c, 8, stride=16), :] = jnp.broadcast_to(
-            top * (1.0 / 32767.0), (8, 128)
-        )
 
     for j, copy in enumerate(exchange):
         copy.wait()
@@ -158,22 +172,24 @@
 
     ends = [lax.rem(z + turned(d, 8, rep), 8) for d in FAR_Z]
 
-    def partners(block):
+    def first_of(block):
         at_y = lax.rem(y + turned(far_x(lax.rem(block, 4)), 4, rep), 4)
         at_x = lax.rem(x + turned(far_x(block // 4), 4, rep), 4)
-        return [at_x * 32 + at_y * 8 + end for end in ends]
+        return at_x * 32 + at_y * 8
+
+    def partners(block):
+        return [first_of(block) + end for end in ends]
 
     def gather(block, found):
         stock = pieces.reshape(N, 8, 128)
         picked = []
         for q in found:
             k = table[rep, q]
-            picked.append((stock[k], scales[pl.ds(k, 1), :]))
-        for u, (word, scale) in enumerate(picked):
+            picked.append(stock[k])
+        for u, word in enumerate(picked):
             out_words[rows(block * 64 + u * 8), :] = word
-            out_scales[block * 8 + u] = scale
-
-    def sends(words, lines, to_words, to_lines, send_sem, recv_sem, plane, forward):
+
+    def sends(words, lines, to_words, to_lines, send_sem, recv_sem, begin, end, forward):
         def one(block, found, count):
             for u, q in enumerate(found[:count]):
                 slot = block * 8 + u if forward else q
@@ -185,6 +201,8 @@
                     device_id=(rep, q),
                     device_id_type=MESH,
                 ).start()
+                if forward:
+                    continue
                 pltpu.make_async_remote_copy(
                     src_ref=lines.at[slot],
                     dst_ref=to_lines.at[me],
@@ -201,19 +219,18 @@
             one(block, found, count)
             return c
 
-        lax.fori_loop(plane * 4, min(plane * 4 + 4, 15), whole, 0)
-        if plane == 3:
+        lax.fori_loop(begin, min(end, 15), whole, 0)
+        if end == 16:
             whole(jnp.int32(15), 0, 7)
 
     others[0].wait()
     pl.semaphore_wait(met, 7)
     for plane in range(4):
         sends(
-            out_words, out_scales, in_words, in_scales,
-            fwd_send, fwd_recv.at[plane], plane, True,
+            out_words, None, in_words, None,
+            fwd_send, fwd_recv.at[plane], plane * 4, plane * 4 + 4, True,
         )
     in_words[rows(me * 8), :] = out_words[rows(8 * (N - 1)), :]
-    in_scales[me] = out_scales[N - 1]
 
     def away(plane):
         return lax.rem(x + 4 - turned(far_x(plane), 4, rep), 4)
@@ -231,25 +248,20 @@
         pltpu.make_async_copy(
             words.at[rows(0, 8 * count)], words.at[rows(0, 8 * count)], sems.at[0]
         ).wait()
+        if lines is None:
+            return
         pltpu.make_async_copy(
             lines.at[pl.ds(0, count)], lines.at[pl.ds(0, count)], sems.at[1]
         ).wait()
 
-    upper = lax.broadcasted_iota(I32, (8, 128), 0) < 4
-
     def decode(j):
-        scale = jnp.where(
-            upper,
-            jnp.broadcast_to(in_scales[2 * j], (8, 128)),
-            jnp.broadcast_to(in_scales[2 * j + 1], (8, 128)),
-        )
         for half in range(2):
             a, b = unpack(in_words[pl.ds(j * 16 + half, 8, stride=2), :])
             for q, col in ((a, half), (b, half + 2)):
-                blocks[rows(j * 8), col * 128 : col * 128 + 128] = q.astype(F32) * scale
+                blocks[rows(j * 8), col * 128 : col * 128 + 128] = log_value(q)
 
     for plane in range(4):
-        arrived(fwd_recv.at[plane], in_words, in_scales, 31 if plane == 3 else 32)
+        arrived(fwd_recv.at[plane], in_words, None, 31 if plane == 3 else 32)
         first = away(plane) * 16
         for j in range(16):
             decode(first + j)
@@ -290,16 +302,20 @@
         ret_scales[2 * j] = scale
         ret_scales[2 * j + 1] = scale
 
-    for plane in range(4):
-        first = lax.rem(x + turned(far_x(plane), 4, rep), 4) * 16
-        some = rows(first * 8, 128)
-        part_left = split(dot3_few((lh[some, :], ll[some, :]), (wh[...], wl[...])))
+    for begin, end in ((0, 2), (2, 4), (4, 8), (8, 12), (12, 16)):
+        firsts = [first_of(block) for block in range(begin, end)]
+        some = [
+            jnp.concatenate([half[rows(first * 4, 32), :] for first in firsts], axis=0)
+            for half in (lh, ll)
+        ]
+        part_left = split(dot3_few(some, (wh[...], wl[...])))
         back = dot3_few(part_left, (rth[...], rtl[...]))
-        for j in range(16):
-            encode(first + j, back[j * 8 : j * 8 + 8, :])
+        for i in range(4 * (end - begin)):
+            j = lax.div(firsts[i // 4], 2) + i % 4
+            encode(j, back[i * 8 : i * 8 + 8, :])
         sends(
             ret_words, ret_scales, back_words, back_scales,
-            bwd_send, bwd_recv, plane, False,
+            bwd_send, bwd_recv, begin, end, False,
         )
     back_words[rows(me * 8), :] = ret_words[rows(me * 8), :]
     back_scales[me] = ret_scales[me]
@@ -308,7 +324,7 @@
     new_left[...] = 0.95 * lf[...] + 0.05 * dot3(pair, pair, ((1,), (1,)))
     new_right[...] = 0.95 * rf[...] + 0.05 * dot3(pair, pair, ((0,), (0,)))
 
-    arrived(fwd_send, out_words, out_scales, N - 1)
+    arrived(fwd_send, out_words, None, N - 1)
     arrived(bwd_send, ret_words, ret_scales, N - 1)
     arrived(bwd_recv, back_words, back_scales, N - 1)
 
@@ -384,13 +400,13 @@
             pltpu.VMEM((4, 8, 8192), F32),
             pltpu.VMEM((2, 16, 8192), BF16),
             pltpu.VMEM((2, 16, 8192), BF16),
-            words, pltpu.VMEM((N, 128), F32), words, lines, words, lines,
+            words, words, words,
             pltpu.VMEM((B, B), F32),
             *halves,
             words, lines,
             pltpu.SemaphoreType.REGULAR,
             dma((CHUNKS,)), dma((7,)), dma((CHUNKS,)), dma((CHUNKS,)),
-            dma((2,)), dma((4, 2)), dma((2,)), dma((2,)),
+            dma((1,)), dma((4, 1)), dma((2,)), dma((2,)),
         ],
         compiler_params=pltpu.CompilerParams(
             collective_id=0, has_side_effects=True, vmem_limit_bytes=49 * 2**20

time: 48.5 us -> 47.2 us (0.973)
  Pallas kernels: 47.1 us -> 45.8 us
    pallas_call x1, Pallas kernels: 44.7 us -> 43.4 us  [body(): pl.pallas_call(step_kernel, out_shape=(jax.ShapeDtypeStruct((N * 8, 128),...]
where the time goes in v1:
time: 47.2 us; the launch traced here: 47.1 us
  Pallas kernels  45.8 us (97%)
  local copies, waits for them, and re-layouts  0.67 us (1%)
  between operations  0.65 us (1%)
    pallas_call x1, Pallas kernels, body(): pl.pallas_call(step_kernel, out_shape=(jax.ShapeDtypeStruct((N * 8, 128),...  43.4 us
    pallas_call x1, Pallas kernels, body(): pl.pallas_call(write_kernel, out_shape=(jax.ShapeDtypeStruct((4, 8, 8192)...  2.4 us

profile of v1, /device:TPU:4, one launch (start us, length us, event | category | flops | bytes accessed | tf_op | source)
XLA Modules:
  0.0 47.1 jit_solution(17712942862024577404)
XLA Ops:
  0.6 0.0 copy-start
  0.6 0.7 %copy-done = s32[2,128]{1,0:T(2,128)S(1)} copy-done((s32[2,128]{1,0:T(2,128)S(1)}, s32[2,128]{1,0:T(2,128)}, u32[]{:S(2)}) %copy-start) | copy-done | bytes 1048
  1.3 43.4 %shard_map.119 = (s32[1024,128]{1,0:T(8,128)S(1)}, f32[128,1,128]{2,1,0:T(1,128)S(1)}, f32[512,512]{1,0:T(8,128)S(1)}, f32[512,512]{1,0:T(8,128)S(1)}, f32[512,512]{1,0:T(8,128)S(1)}, /*index=5*/f32[512,512]{1,0:T(8,128)S(1)}) custom-call(bf16[1,4,16,8192]{3,2,1,0:T(8,128)(2,1)} %g_hbm.1, f32[1,512,512]{2,1,0:T(8,128)} %l_hbm.1, f32[1,512,512]{2,1,0:T(8,128)} %r_hbm.1, ...), custom_call_target="tpu_custom_call" | custom-call | tf_op jit(solution)/shard_map/pallas_call | solution.py:387
  44.7 2.4 %shard_map.120 = (f32[4,8,8192]{2,1,0:T(8,128)}, f32[1,512,512]{2,1,0:T(8,128)}, f32[1,512,512]{2,1,0:T(8,128)}, f32[1,512,512]{2,1,0:T(8,128)}, f32[1,512,512]{2,1,0:T(8,128)}) custom-call(s32[1024,128]{1,0:T(8,128)S(1)} %get-tuple-element.11.words, f32[128,1,128]{2,1,0:T(1,128)S(1)} %get-tuple-element.12.lines, f32[512,512]{1,0:T(8,128)S(1)} %get-tuple-element.13.first, ...), custom_call_target="tpu_custom_call" | custom-call | tf_op jit(solution)/shard_map/pallas_call | solution.py:416
Async XLA Ops:
  0.6 0.7 %copy-start = (s32[2,128]{1,0:T(2,128)S(1)}, s32[2,128]{1,0:T(2,128)}, u32[]{:S(2)}) copy-start(s32[2,128]{1,0:T(2,128)} %table_hbm.3) | copy-start | bytes 3076

commit v2 on v1

--- a/solution.py
+++ b/solution.py
@@ -23,6 +23,10 @@
 
 def far_x(plane):
     return jnp.where(plane == 0, 2, jnp.where(plane == 3, 0, 2 * plane - 1))
+
+
+def near_x(plane):
+    return jnp.where(plane == 3, 0, plane + 1)
 
 
 def turned(step, size, rep):
@@ -174,7 +178,7 @@
 
     def first_of(block):
         at_y = lax.rem(y + turned(far_x(lax.rem(block, 4)), 4, rep), 4)
-        at_x = lax.rem(x + turned(far_x(block // 4), 4, rep), 4)
+        at_x = lax.rem(x + turned(near_x(block // 4), 4, rep), 4)
         return at_x * 32 + at_y * 8
 
     def partners(block):
@@ -233,7 +237,7 @@
     in_words[rows(me * 8), :] = out_words[rows(8 * (N - 1)), :]
 
     def away(plane):
-        return lax.rem(x + 4 - turned(far_x(plane), 4, rep), 4)
+        return lax.rem(x + 4 - turned(near_x(plane), 4, rep), 4)
 
     for copy in others[1:]:
         copy.wait()

time: 47.2 us -> 47.2 us (level)
  no operation moved by 1% of the time
where the time goes in v2:
time: 47.2 us; the launch traced here: 47.1 us
  Pallas kernels  45.8 us (97%)
  local copies, waits for them, and re-layouts  0.67 us (1%)
  between operations  0.65 us (1%)
    pallas_call x1, Pallas kernels, body(): pl.pallas_call(step_kernel, out_shape=(jax.ShapeDtypeStruct((N * 8, 128),...  43.4 us
    pallas_call x1, Pallas kernels, body(): pl.pallas_call(write_kernel, out_shape=(jax.ShapeDtypeStruct((4, 8, 8192)...  2.4 us

profile of v2, /device:TPU:4, one launch (start us, length us, event | category | flops | bytes accessed | tf_op | source)
XLA Modules:
  0.0 47.1 jit_solution(5990625311852727249)
XLA Ops:
  0.6 0.0 copy-start
  0.6 0.7 %copy-done = s32[2,128]{1,0:T(2,128)S(1)} copy-done((s32[2,128]{1,0:T(2,128)S(1)}, s32[2,128]{1,0:T(2,128)}, u32[]{:S(2)}) %copy-start) | copy-done | bytes 1048
  1.3 43.4 %shard_map.119 = (s32[1024,128]{1,0:T(8,128)S(1)}, f32[128,1,128]{2,1,0:T(1,128)S(1)}, f32[512,512]{1,0:T(8,128)S(1)}, f32[512,512]{1,0:T(8,128)S(1)}, f32[512,512]{1,0:T(8,128)S(1)}, /*index=5*/f32[512,512]{1,0:T(8,128)S(1)}) custom-call(bf16[1,4,16,8192]{3,2,1,0:T(8,128)(2,1)} %g_hbm.1, f32[1,512,512]{2,1,0:T(8,128)} %l_hbm.1, f32[1,512,512]{2,1,0:T(8,128)} %r_hbm.1, ...), custom_call_target="tpu_custom_call" | custom-call | tf_op jit(solution)/shard_map/pallas_call | solution.py:391
  44.7 2.4 %shard_map.120 = (f32[4,8,8192]{2,1,0:T(8,128)}, f32[1,512,512]{2,1,0:T(8,128)}, f32[1,512,512]{2,1,0:T(8,128)}, f32[1,512,512]{2,1,0:T(8,128)}, f32[1,512,512]{2,1,0:T(8,128)}) custom-call(s32[1024,128]{1,0:T(8,128)S(1)} %get-tuple-element.11.words, f32[128,1,128]{2,1,0:T(1,128)S(1)} %get-tuple-element.12.lines, f32[512,512]{1,0:T(8,128)S(1)} %get-tuple-element.13.first, ...), custom_call_target="tpu_custom_call" | custom-call | tf_op jit(solution)/shard_map/pallas_call | solution.py:420
Async XLA Ops:
  0.6 0.7 %copy-start = (s32[2,128]{1,0:T(2,128)S(1)}, s32[2,128]{1,0:T(2,128)}, u32[]{:S(2)}) copy-start(s32[2,128]{1,0:T(2,128)} %table_hbm.3) | copy-start | bytes 3076
